TPU v7x, 512 devices: a whole 4x4x16 slice. The times are simulated.
512 devices in a mesh: ctx: 128 (over z, y, core), tp: 4 (over x).
Axes of the slice: x: 4, y: 4, z: 16, core: 2. Of those that a mesh axis runs over, the one named last changes fastest.
Arguments:
- query: bfloat16 [32768, 4096], P('ctx', 'tp'), may hold values from -6 to 6
- key: bfloat16 [32768, 4096], P('ctx', 'tp'), may hold values from -6 to 6
- value: bfloat16 [32768, 4096], P('ctx', 'tp'), may hold values from -68 to 68
- gain: float32 [4096], P('tp'), may hold values from 0.1 to 1.9
- grad_out: bfloat16 [32768, 4096], P('ctx', 'tp'), may hold values from -6 to 6
Outputs:
- grad_query: bfloat16 [32768, 4096], P('ctx', 'tp')
- grad_key: bfloat16 [32768, 4096], P('ctx', 'tp')
- grad_value: bfloat16 [32768, 4096], P('ctx', 'tp')
All inputs are finite; a program needn't handle non-finite values.
Results may differ from a plain program's by a relative error of at most 0.0065.
Values sent between devices are 32-bit elements; how exact they have to be, the bound alone decides.
A program may use at most 64 MiB of HBM per device.

v0:
```python
import jax
import jax.numpy as jnp
from jax import lax
from jax.sharding import PartitionSpec as P

HEAD = 128
BLOCK = 256


def passed_along(value, axis, steps):
    count = lax.axis_size(axis)
    initial, last = (max(0, -steps), min(count, count - steps))
    return lax.ppermute(value, axis, [(source, source + steps) for source in range(initial, last)])


def unit_rows(raw, rows, heads):
    wide = raw.astype(jnp.float32).reshape(rows, heads, HEAD)
    length = jnp.sqrt(jnp.sum(wide * wide, -1, keepdims=True) + 1e-06)
    return (wide / length, length)


def project_back(grad, unit, length):
    return (grad - unit * jnp.sum(unit * grad, -1, keepdims=True)) / length


def levels_of(count):
    return (count - 1).bit_length()


def kv_before(own):
    total = own
    for level in range(levels_of(lax.axis_size("ctx"))):
        total = total + passed_along(total, "ctx", 1 << level)
    return total - own


def qd_after(own):
    total = own
    for level in range(levels_of(lax.axis_size("ctx"))):
        total = total + passed_along(total, "ctx", -(1 << level))
    return total - own


def body(query, key, value, gain, grad_out):
    top = lax.Precision.HIGHEST
    f32 = jnp.float32
    rows, width = query.shape
    heads = width // HEAD
    count = rows // BLOCK
    shape4 = (count, BLOCK, heads, HEAD)
    q_unit, q_norm = unit_rows(query, rows, heads)
    k_unit, k_norm = unit_rows(key, rows, heads)
    q_b = q_unit.astype(jnp.bfloat16).reshape(shape4)
    k_b = k_unit.astype(jnp.bfloat16).reshape(shape4)
    v_b = value.reshape(shape4)
    lower = jnp.tril(jnp.ones((BLOCK, BLOCK), f32))
    outer_kv = jnp.einsum("nshd,nshe->nhde", k_b, v_b, preferred_element_type=f32)
    before = kv_before(jnp.sum(outer_kv, 0))
    prior = before[None] + (jnp.cumsum(outer_kv, 0) - outer_kv)
    scores = jnp.einsum("nthd,nshd->nhts", q_b, k_b, preferred_element_type=f32) * lower
    scores_b = scores.astype(jnp.bfloat16)
    attended = jnp.einsum("nhts,nshe->nthe", scores_b, v_b, preferred_element_type=f32)
    attended = attended + jnp.einsum("nthd,nhde->nthe", q_b.astype(f32), prior, precision=top)
    flat = attended.reshape(rows, width)
    weighted = grad_out.astype(f32) * gain
    sq_sum, cross = lax.psum((jnp.sum(flat * flat, -1), jnp.sum(weighted * flat, -1)), "tp")
    full = width * lax.axis_size("tp")
    rms = jnp.sqrt(sq_sum / full + 1e-05)
    d_att = weighted / rms[:, None] - flat * (cross / (full * rms * rms * rms))[:, None]
    d_b = d_att.astype(jnp.bfloat16).reshape(shape4)
    outer_qd = jnp.einsum("nthd,nthe->nhde", q_b, d_b, preferred_element_type=f32)
    own = jnp.sum(outer_qd, 0)
    after = qd_after(own)
    suffix = jnp.flip(jnp.cumsum(jnp.flip(outer_qd, 0), 0), 0)
    later = after[None] + (suffix - outer_qd)
    d_scores_b = (
        jnp.einsum("nthe,nshe->nhts", d_b, v_b, preferred_element_type=f32) * lower
    ).astype(jnp.bfloat16)
    d_q = jnp.einsum("nhts,nshd->nthd", d_scores_b, k_b, preferred_element_type=f32)
    d_q = d_q + jnp.einsum("nthe,nhde->nthd", d_b.astype(f32), prior, precision=top)
    d_k = jnp.einsum("nhts,nthd->nshd", d_scores_b, q_b, preferred_element_type=f32)
    d_k = d_k + jnp.einsum("nshe,nhde->nshd", v_b.astype(f32), later, precision=top)
    d_v = jnp.einsum("nhts,nthe->nshe", scores_b, d_b, preferred_element_type=f32)
    d_v = d_v + jnp.einsum("nshd,nhde->nshe", k_b.astype(f32), later, precision=top)
    grad_query = project_back(d_q.reshape(rows, heads, HEAD), q_unit, q_norm)
    grad_key = project_back(d_k.reshape(rows, heads, HEAD), k_unit, k_norm)
    return (
        grad_query.reshape(rows, width).astype(jnp.bfloat16),
        grad_key.reshape(rows, width).astype(jnp.bfloat16),
        d_v.reshape(rows, width).astype(jnp.bfloat16),
    )


def solution(mesh):
    placed = (P("ctx", "tp"), P("ctx", "tp"), P("ctx", "tp"), P("tp"), P("ctx", "tp"))
    return jax.shard_map(
        body,
        mesh=mesh,
        in_specs=placed,
        out_specs=(P("ctx", "tp"), P("ctx", "tp"), P("ctx", "tp")),
        check_vma=False,
    )
```

profile of v0, /device:TPU:33, one launch (start us, length us, event | category | flops | bytes accessed | tf_op | source)
XLA Modules:
  0.0 409.0 jit_solution(787160006987535757)
XLA Ops:
  0.6 1.3 copy.33
  3.2 3.8 collective-permute-start
  7.0 6.1 %collective-permute-done = f32[8,128,128]{2,1,0:T(8,128)S(1)} collective-permute-done((f32[8,128,128]{2,1,0:T(8,128)S(1)}, f32[8,128,128]{2,1,0:T(8,128)S(1)}, u32[]{:S(2)}, u32[]{:S(2)}) %collective-permute-start) | collective-permute-done | bytes 524320 | tf_op jit(solution)/shard_map/ppermute | solution.py:13
  13.2 3.2 collective-permute-start.1
  16.4 10.8 %collective-permute-done.1 = f32[8,128,128]{2,1,0:T(8,128)S(1)} collective-permute-done((f32[8,128,128]{2,1,0:T(8,128)S(1)}, f32[8,128,128]{2,1,0:T(8,128)S(1)}, u32[]{:S(2)}, u32[]{:S(2)}) %collective-permute-start.1) | collective-permute-done | bytes 524320 | tf_op jit(solution)/shard_map/ppermute | solution.py:13
  27.3 4.2 %collective-permute-start.2 = (f32[8,128,128]{2,1,0:T(8,128)S(1)}, f32[8,128,128]{2,1,0:T(8,128)S(1)}, u32[]{:S(2)}, u32[]{:S(2)}) collective-permute-start(f32[8,128,128]{2,1,0:T(8,128)S(1)} %add.115), channel_id=1, source_target_pairs={{0,16},{4,20},{8,24},{12,28},{16,32},{20,36},{24,40},{28,44},{32,4... | collective-permute-start | bytes 1572872 | tf_op jit(solution)/shard_map/ppermute | solution.py:13
  31.5 9.1 %collective-permute-done.2 = f32[8,128,128]{2,1,0:T(8,128)S(1)} collective-permute-done((f32[8,128,128]{2,1,0:T(8,128)S(1)}, f32[8,128,128]{2,1,0:T(8,128)S(1)}, u32[]{:S(2)}, u32[]{:S(2)}) %collective-permute-start.2) | collective-permute-done | bytes 524320 | tf_op jit(solution)/shard_map/ppermute | solution.py:13
  40.7 3.5 collective-permute-start.3
  44.2 6.4 %collective-permute-done.3 = f32[8,128,128]{2,1,0:T(8,128)S(1)} collective-permute-done((f32[8,128,128]{2,1,0:T(8,128)S(1)}, f32[8,128,128]{2,1,0:T(8,128)S(1)}, u32[]{:S(2)}, u32[]{:S(2)}) %collective-permute-start.3) | collective-permute-done | bytes 524320 | tf_op jit(solution)/shard_map/ppermute | solution.py:13
  50.7 12.2 %collective-permute-start.4 = (f32[8,128,128]{2,1,0:T(8,128)S(1)}, f32[8,128,128]{2,1,0:T(8,128)}, u32[]{:S(2)}, u32[]{:S(2)}) collective-permute-start(f32[8,128,128]{2,1,0:T(8,128)S(1)} %add.117), channel_id=1, source_target_pairs={{0,64},{4,68},{8,72},{12,76},{16,80},{20,84},{24,88},{28,92},{32,9... | collective-permute-start | bytes 1572872 | tf_op jit(solution)/shard_map/ppermute | solution.py:13
  64.2 19.7 %collective-permute-done.4 = f32[8,128,128]{2,1,0:T(8,128)} collective-permute-done((f32[8,128,128]{2,1,0:T(8,128)S(1)}, f32[8,128,128]{2,1,0:T(8,128)}, u32[]{:S(2)}, u32[]{:S(2)}) %collective-permute-start.4) | collective-permute-done | bytes 524320 | tf_op jit(solution)/shard_map/ppermute | solution.py:13
  85.1 1.3 collective-permute-start.5
  86.5 16.7 %collective-permute-done.5 = f32[8,128,128]{2,1,0:T(8,128)S(1)} collective-permute-done((f32[8,128,128]{2,1,0:T(8,128)S(1)}, f32[8,128,128]{2,1,0:T(8,128)S(1)}, u32[]{:S(2)}, u32[]{:S(2)}) %collective-permute-start.5) | collective-permute-done | bytes 524320 | tf_op jit(solution)/shard_map/ppermute | solution.py:13
  103.3 7.4 %collective-permute-start.6 = (f32[8,128,128]{2,1,0:T(8,128)S(1)}, f32[8,128,128]{2,1,0:T(8,128)S(1)}, u32[]{:S(2)}, u32[]{:S(2)}) collective-permute-start(f32[8,128,128]{2,1,0:T(8,128)S(1)} %add.119), channel_id=1, source_target_pairs={{0,256},{4,260},{8,264},{12,268},{16,272},{20,276},{24,280},{28,28... | collective-permute-start | bytes 1572872 | tf_op jit(solution)/shard_map/ppermute | solution.py:13
  112.1 4.6 %collective-permute-done.6 = f32[8,128,128]{2,1,0:T(8,128)S(1)} collective-permute-done((f32[8,128,128]{2,1,0:T(8,128)S(1)}, f32[8,128,128]{2,1,0:T(8,128)S(1)}, u32[]{:S(2)}, u32[]{:S(2)}) %collective-permute-start.6) | collective-permute-done | bytes 524320 | tf_op jit(solution)/shard_map/ppermute | solution.py:13
  116.7 1.7 fusion.9
  118.5 2.6 copy.42
  121.1 1.4 multiply_reduce_fusion
  122.5 8.5 %all-reduce = (f32[256]{0:T(256)S(1)}, f32[256]{0:T(256)S(1)}) all-reduce(f32[256]{0:T(256)S(1)} %multiply_reduce_fusion, f32[256]{0:T(256)S(1)} %get-tuple-element.13), channel_id=1, replica_groups=mesh['ctx'=128,'tp'=4] {'tp'}, use_global_device_ids=true, to_apply=%region_5.6 | all-reduce | flops 512 | bytes 4096 | tf_op jit(solution)/shard_map/psum | solution.py:66
  131.0 2.3 subtract_convert_fusion
  133.2 1.2 copy.66
  134.8 21.5 %collective-permute-start.7 = (f32[8,128,128]{2,1,0:T(8,128)S(1)}, f32[8,128,128]{2,1,0:T(8,128)S(1)}, u32[]{:S(2)}, u32[]{:S(2)}) collective-permute-start(f32[8,128,128]{2,1,0:T(8,128)S(1)} %fusion.25), channel_id=1, source_target_pairs={{4,0},{8,4},{12,8},{16,12},{20,16},{24,20},{28,24},{32,28},{36,32}... | collective-permute-start | bytes 1572872 | tf_op jit(solution)/shard_map/ppermute | solution.py:13
  156.3 53.6 %collective-permute-done.7 = f32[8,128,128]{2,1,0:T(8,128)S(1)} collective-permute-done((f32[8,128,128]{2,1,0:T(8,128)S(1)}, f32[8,128,128]{2,1,0:T(8,128)S(1)}, u32[]{:S(2)}, u32[]{:S(2)}) %collective-permute-start.7) | collective-permute-done | bytes 524320 | tf_op jit(solution)/shard_map/ppermute | solution.py:13
  210.0 1.9 collective-permute-start.8
  212.0 12.3 %collective-permute-done.8 = f32[8,128,128]{2,1,0:T(8,128)S(1)} collective-permute-done((f32[8,128,128]{2,1,0:T(8,128)S(1)}, f32[8,128,128]{2,1,0:T(8,128)S(1)}, u32[]{:S(2)}, u32[]{:S(2)}) %collective-permute-start.8) | collective-permute-done | bytes 524320 | tf_op jit(solution)/shard_map/ppermute | solution.py:13
  224.3 3.1 collective-permute-start.9
  227.5 13.8 %collective-permute-done.9 = f32[8,128,128]{2,1,0:T(8,128)S(1)} collective-permute-done((f32[8,128,128]{2,1,0:T(8,128)S(1)}, f32[8,128,128]{2,1,0:T(8,128)S(1)}, u32[]{:S(2)}, u32[]{:S(2)}) %collective-permute-start.9) | collective-permute-done | bytes 524320 | tf_op jit(solution)/shard_map/ppermute | solution.py:13
  242.1 1.9 collective-permute-start.10
  245.1 2.5 copy.46
  248.7 2.6 copy.52
  251.2 6.2 %collective-permute-done.10 = f32[8,128,128]{2,1,0:T(8,128)} collective-permute-done((f32[8,128,128]{2,1,0:T(8,128)}, f32[8,128,128]{2,1,0:T(8,128)}, u32[]{:S(2)}, u32[]{:S(2)}) %collective-permute-start.10) | collective-permute-done | bytes 524320 | tf_op jit(solution)/shard_map/ppermute | solution.py:13
  257.4 1.3 add.133
  258.7 1.4 collective-permute-start.11
  260.6 1.3 fusion.26
  261.9 24.4 %collective-permute-done.11 = f32[8,128,128]{2,1,0:T(8,128)S(1)} collective-permute-done((f32[8,128,128]{2,1,0:T(8,128)S(1)}, f32[8,128,128]{2,1,0:T(8,128)S(1)}, u32[]{:S(2)}, u32[]{:S(2)}) %collective-permute-start.11) | collective-permute-done | bytes 524320 | tf_op jit(solution)/shard_map/ppermute | solution.py:13
  286.5 1.4 collective-permute-start.12
  288.4 1.8 fusion.8
  290.2 20.2 %collective-permute-done.12 = f32[8,128,128]{2,1,0:T(8,128)S(1)} collective-permute-done((f32[8,128,128]{2,1,0:T(8,128)S(1)}, f32[8,128,128]{2,1,0:T(8,128)S(1)}, u32[]{:S(2)}, u32[]{:S(2)}) %collective-permute-start.12) | collective-permute-done | bytes 524320 | tf_op jit(solution)/shard_map/ppermute | solution.py:13
  310.5 1.6 collective-permute-start.13
  312.1 1.3 fusion.24
  313.4 1.4 copy.48
  316.1 2.8 fusion.6
  318.9 78.3 %collective-permute-done.13 = f32[8,128,128]{2,1,0:T(8,128)} collective-permute-done((f32[8,128,128]{2,1,0:T(8,128)S(1)}, f32[8,128,128]{2,1,0:T(8,128)}, u32[]{:S(2)}, u32[]{:S(2)}) %collective-permute-start.13) | collective-permute-done | bytes 524320 | tf_op jit(solution)/shard_map/ppermute | solution.py:13
  397.2 2.5 fusion
  399.7 2.1 copy.59
  401.8 3.1 fusion.7
  404.9 1.6 copy.54
  407.7 1.3 fusion.3
  (72 shorter events, 12.7 us)
Async XLA Ops:
  0.6 2.3 copy-start
  2.0 1.0 copy-start.1
  3.2 113.5 %copy-start.5 = (f32[8,128,128]{2,1,0:T(8,128)}, f32[8,128,128]{2,1,0:T(8,128)S(1)}, u32[]{:S(2)}) copy-start(f32[8,128,128]{2,1,0:T(8,128)S(1)} %fusion.13) | copy-start | bytes 1572868
  3.2 9.9 %collective-permute-start = (f32[8,128,128]{2,1,0:T(8,128)S(1)}, f32[8,128,128]{2,1,0:T(8,128)S(1)}, u32[]{:S(2)}, u32[]{:S(2)}) collective-permute-start(f32[8,128,128]{2,1,0:T(8,128)S(1)} %fusion.13), channel_id=1, source_target_pairs={{0,4},{4,8},{8,12},{12,16},{16,20},{20,24},{24,28},{28,32},{32,36}... | collective-permute-start | bytes 1572872 | tf_op jit(solution)/shard_map/ppermute | solution.py:13
  13.2 14.0 %collective-permute-start.1 = (f32[8,128,128]{2,1,0:T(8,128)S(1)}, f32[8,128,128]{2,1,0:T(8,128)S(1)}, u32[]{:S(2)}, u32[]{:S(2)}) collective-permute-start(f32[8,128,128]{2,1,0:T(8,128)S(1)} %add.114), channel_id=1, source_target_pairs={{0,8},{4,12},{8,16},{12,20},{16,24},{20,28},{24,32},{28,36},{32,40... | collective-permute-start | bytes 1572872 | tf_op jit(solution)/shard_map/ppermute | solution.py:13
  27.3 13.4 %collective-permute-start.2 = (f32[8,128,128]{2,1,0:T(8,128)S(1)}, f32[8,128,128]{2,1,0:T(8,128)S(1)}, u32[]{:S(2)}, u32[]{:S(2)}) collective-permute-start(f32[8,128,128]{2,1,0:T(8,128)S(1)} %add.115), channel_id=1, source_target_pairs={{0,16},{4,20},{8,24},{12,28},{16,32},{20,36},{24,40},{28,44},{32,4... | collective-permute-start | bytes 1572872 | tf_op jit(solution)/shard_map/ppermute | solution.py:13
  40.7 9.9 %collective-permute-start.3 = (f32[8,128,128]{2,1,0:T(8,128)S(1)}, f32[8,128,128]{2,1,0:T(8,128)S(1)}, u32[]{:S(2)}, u32[]{:S(2)}) collective-permute-start(f32[8,128,128]{2,1,0:T(8,128)S(1)} %add.116), channel_id=1, source_target_pairs={{0,32},{4,36},{8,40},{12,44},{16,48},{20,52},{24,56},{28,60},{32,6... | collective-permute-start | bytes 1572872 | tf_op jit(solution)/shard_map/ppermute | solution.py:13
  50.7 33.3 %collective-permute-start.4 = (f32[8,128,128]{2,1,0:T(8,128)S(1)}, f32[8,128,128]{2,1,0:T(8,128)}, u32[]{:S(2)}, u32[]{:S(2)}) collective-permute-start(f32[8,128,128]{2,1,0:T(8,128)S(1)} %add.117), channel_id=1, source_target_pairs={{0,64},{4,68},{8,72},{12,76},{16,80},{20,84},{24,88},{28,92},{32,9... | collective-permute-start | bytes 1572872 | tf_op jit(solution)/shard_map/ppermute | solution.py:13
  85.1 18.1 %collective-permute-start.5 = (f32[8,128,128]{2,1,0:T(8,128)S(1)}, f32[8,128,128]{2,1,0:T(8,128)S(1)}, u32[]{:S(2)}, u32[]{:S(2)}) collective-permute-start(f32[8,128,128]{2,1,0:T(8,128)S(1)} %add.118), channel_id=1, source_target_pairs={{0,128},{4,132},{8,136},{12,140},{16,144},{20,148},{24,152},{28,15... | collective-permute-start | bytes 1572872 | tf_op jit(solution)/shard_map/ppermute | solution.py:13
  103.3 13.5 %copy-start.9 = (f32[8,128,128]{2,1,0:T(8,128)}, f32[8,128,128]{2,1,0:T(8,128)S(1)}, u32[]{:S(2)}) copy-start(f32[8,128,128]{2,1,0:T(8,128)S(1)} %add.119) | copy-start | bytes 1572868
  103.3 13.5 %collective-permute-start.6 = (f32[8,128,128]{2,1,0:T(8,128)S(1)}, f32[8,128,128]{2,1,0:T(8,128)S(1)}, u32[]{:S(2)}, u32[]{:S(2)}) collective-permute-start(f32[8,128,128]{2,1,0:T(8,128)S(1)} %add.119), channel_id=1, source_target_pairs={{0,256},{4,260},{8,264},{12,268},{16,272},{20,276},{24,280},{28,28... | collective-permute-start | bytes 1572872 | tf_op jit(solution)/shard_map/ppermute | solution.py:13
  111.1 1.0 copy-start.3
  116.7 1.7 copy-start.15
  118.5 2.6 copy-start.17
  118.5 2.6 copy-start.19
  134.8 89.5 %copy-start.7 = (f32[8,128,128]{2,1,0:T(8,128)}, f32[8,128,128]{2,1,0:T(8,128)S(1)}, u32[]{:S(2)}) copy-start(f32[8,128,128]{2,1,0:T(8,128)S(1)} %fusion.25) | copy-start | bytes 1572868
  134.8 75.2 %collective-permute-start.7 = (f32[8,128,128]{2,1,0:T(8,128)S(1)}, f32[8,128,128]{2,1,0:T(8,128)S(1)}, u32[]{:S(2)}, u32[]{:S(2)}) collective-permute-start(f32[8,128,128]{2,1,0:T(8,128)S(1)} %fusion.25), channel_id=1, source_target_pairs={{4,0},{8,4},{12,8},{16,12},{20,16},{24,20},{28,24},{32,28},{36,32}... | collective-permute-start | bytes 1572872 | tf_op jit(solution)/shard_map/ppermute | solution.py:13
  210.0 14.2 %collective-permute-start.8 = (f32[8,128,128]{2,1,0:T(8,128)S(1)}, f32[8,128,128]{2,1,0:T(8,128)S(1)}, u32[]{:S(2)}, u32[]{:S(2)}) collective-permute-start(f32[8,128,128]{2,1,0:T(8,128)S(1)} %add.130), channel_id=1, source_target_pairs={{8,0},{12,4},{16,8},{20,12},{24,16},{28,20},{32,24},{36,28},{40,32... | collective-permute-start | bytes 1572872 | tf_op jit(solution)/shard_map/ppermute | solution.py:13
  224.3 16.9 %collective-permute-start.9 = (f32[8,128,128]{2,1,0:T(8,128)S(1)}, f32[8,128,128]{2,1,0:T(8,128)S(1)}, u32[]{:S(2)}, u32[]{:S(2)}) collective-permute-start(f32[8,128,128]{2,1,0:T(8,128)S(1)} %add.131), channel_id=1, source_target_pairs={{16,0},{20,4},{24,8},{28,12},{32,16},{36,20},{40,24},{44,28},{48,3... | collective-permute-start | bytes 1572872 | tf_op jit(solution)/shard_map/ppermute | solution.py:13
  242.1 15.3 %collective-permute-start.10 = (f32[8,128,128]{2,1,0:T(8,128)}, f32[8,128,128]{2,1,0:T(8,128)}, u32[]{:S(2)}, u32[]{:S(2)}) collective-permute-start(f32[8,128,128]{2,1,0:T(8,128)} %add.132), channel_id=1, source_target_pairs={{32,0},{36,4},{40,8},{44,12},{48,16},{52,20},{56,24},{60,28},{64,3... | collective-permute-start | bytes 1572872 | tf_op jit(solution)/shard_map/ppermute | solution.py:13
  258.7 1.9 copy-start.4
  258.7 27.7 %collective-permute-start.11 = (f32[8,128,128]{2,1,0:T(8,128)S(1)}, f32[8,128,128]{2,1,0:T(8,128)S(1)}, u32[]{:S(2)}, u32[]{:S(2)}) collective-permute-start(f32[8,128,128]{2,1,0:T(8,128)S(1)} %add.133), channel_id=1, source_target_pairs={{64,0},{68,4},{72,8},{76,12},{80,16},{84,20},{88,24},{92,28},{96,3... | collective-permute-start | bytes 1572872 | tf_op jit(solution)/shard_map/ppermute | solution.py:13
  286.4 1.9 copy-start.6
  286.5 1.9 copy-start.10
  286.5 1.9 copy-start.16
  286.5 23.9 %collective-permute-start.12 = (f32[8,128,128]{2,1,0:T(8,128)S(1)}, f32[8,128,128]{2,1,0:T(8,128)S(1)}, u32[]{:S(2)}, u32[]{:S(2)}) collective-permute-start(f32[8,128,128]{2,1,0:T(8,128)S(1)} %add.134), channel_id=1, source_target_pairs={{128,0},{132,4},{136,8},{140,12},{144,16},{148,20},{152,24},{156,2... | collective-permute-start | bytes 1572872 | tf_op jit(solution)/shard_map/ppermute | solution.py:13
  310.5 2.9 copy-start.12
  310.5 86.7 %collective-permute-start.13 = (f32[8,128,128]{2,1,0:T(8,128)S(1)}, f32[8,128,128]{2,1,0:T(8,128)}, u32[]{:S(2)}, u32[]{:S(2)}) collective-permute-start(f32[8,128,128]{2,1,0:T(8,128)S(1)} %add.135), channel_id=1, source_target_pairs={{256,0},{260,4},{264,8},{268,12},{272,16},{276,20},{280,24},{284,2... | collective-permute-start | bytes 1572872 | tf_op jit(solution)/shard_map/ppermute | solution.py:13
  314.9 1.2 copy-start.14
  316.1 81.1 %copy-start.8 = (f32[8,128,128]{2,1,0:T(8,128)S(1)}, f32[8,128,128]{2,1,0:T(8,128)}, u32[]{:S(2)}) copy-start(f32[8,128,128]{2,1,0:T(8,128)} %copy-done.7) | copy-start | bytes 1572868
  316.1 81.1 %copy-start.11 = (f32[8,128,256]{2,1,0:T(8,128)S(1)}, f32[8,128,256]{2,1,0:T(8,128)}, u32[]{:S(2)}) copy-start(f32[8,128,256]{2,1,0:T(8,128)} %fusion.26) | copy-start | bytes 3145732
  399.7 2.1 copy-start.2
  404.9 2.1 copy-start.18
  406.5 1.2 copy-start.13
where the time goes:
time: 410 us; the launch traced here: 409 us
  waiting for transfers between devices  282 us (69%)
  starting transfers between devices  68.6 us (17%)
  local copies, waits for them, and re-layouts  22.6 us (6%)
  matrix products  14.1 us (3%)
  other arithmetic  12 us (3%)
  blocking collectives  8.46 us (2%)
    ppermute x14, waiting for transfers between devices, passed_along(): lax.ppermute(value, axis, [(source, source + steps) for source in range(i...  282 us
    ppermute x14, starting transfers between devices, passed_along(): lax.ppermute(value, axis, [(source, source + steps) for source in range(i...  68.6 us
    psum x1, blocking collectives, body(): lax.psum((jnp.sum(flat * flat, -1), jnp.sum(weighted * flat, -1)), 'tp')  8.46 us
  transfers between devices with their start and end apart: 14, of which 14 were waited for; matrix products, arithmetic and copies ran while one was open for 5% of the time, Pallas kernels for 0%

commit v1 on v0

v1 whole, which is shorter than its diff:
```python
import jax
import jax.numpy as jnp
from jax import lax
from jax.experimental import pallas as pl
from jax.experimental.pallas import tpu as pltpu
from jax.sharding import PartitionSpec as P

HEAD = 128
BLOCK = 256
HEADS = 8
HALF = 4
NY = 4
NZ = 16
NX = 4
ROWS = HEAD // NZ
F32 = jnp.float32
BF16 = jnp.bfloat16
MESH = pl.DeviceIdType.MESH
FAR_FIRST = sorted(range(1, NZ), key=lambda d: -min(d, NZ - d))

NN = (((1,), (0,)), ((), ()))
NT = (((1,), (1,)), ((), ()))
TN = (((0,), (0,)), ((), ()))


def dot(a, b, dims):
    return lax.dot_general(a, b, dims, preferred_element_type=F32)


def split(wide, axis):
    high = wide.astype(BF16)
    low = (wide - high.astype(F32)).astype(BF16)
    return jnp.concatenate([high, low], axis)


def twice(narrow):
    return jnp.concatenate([narrow, narrow], 1)


class Place:
    def __init__(self):
        ctx = lax.axis_index("ctx")
        self.x = lax.axis_index("tp")
        self.z = lax.div(ctx, 2 * NY)
        self.y = lax.rem(lax.div(ctx, 2), NY)
        self.core = lax.rem(ctx, 2)

    def at(self, z=None, y=None, core=None, x=None):
        z = self.z if z is None else z
        y = self.y if y is None else y
        core = self.core if core is None else core
        x = self.x if x is None else x
        return ((z * NY + y) * 2 + core, x)


def remote(src, dst, send, recv, device):
    return pltpu.make_async_remote_copy(
        src_ref=src, dst_ref=dst, send_sem=send, recv_sem=recv, device_id=device, device_id_type=MESH
    )


class Scan:
    def __init__(self, me, state, bufs, reverse):
        (self.other, self.chip, self.plane, self.ahead, self.total, self.planes, self.sums, self.base,
         self.out, self.mine, self.fore, self.result, self.sems) = bufs
        self.me, self.state, self.reverse = me, state, reverse
        self.sends = []

    def sem(self, slot):
        return self.sems.at[0, slot], self.sems.at[1, slot]

    def order(self, count):
        return reversed(range(count)) if self.reverse else range(count)

    def go(self, copy):
        copy.start()
        self.sends.append(copy)
        return copy

    def head_copy(self, d):
        me = self.me
        s = lax.rem(me.y + d, NY)
        return remote(
            self.state.at[HALF * (1 - me.core) + s], self.other.at[s], *self.sem(d), me.at(core=1 - me.core)
        )

    def send_head(self, d):
        self.go(self.head_copy(d))

    def y_phase(self):
        me = self.me
        waits = []
        for d in (1, 2, 3, 0):
            s = lax.rem(me.y + d, NY)
            self.head_copy(d).wait_recv()
            whole = self.state[HALF * me.core + s] + self.other[s]
            if d:
                self.chip[s] = whole
                waits.append(self.go(remote(
                    self.chip.at[s], self.plane.at[me.y], *self.sem(4 + d), me.at(y=s)
                )))
            else:
                self.plane[s] = whole
        for copy in waits:
            copy.wait_recv()
        run = jnp.zeros((HEAD, HEAD), F32)
        for y in self.order(NY):
            self.ahead[y] = run
            run = run + self.plane[y]
        self.total[...] = run.reshape(NZ, ROWS, HEAD)

    def z_send(self):
        me = self.me
        self.z_waits = []
        for d in FAR_FIRST:
            z = lax.rem(me.z + d, NZ)
            self.z_waits.append(self.go(remote(
                self.total.at[z], self.planes.at[me.z], *self.sem(8 + d), me.at(z=z)
            )))
        self.planes[me.z] = self.total[me.z]

    def z_back(self):
        me = self.me
        for copy in self.z_waits:
            copy.wait_recv()
        run = jnp.zeros((ROWS, HEAD), F32)
        for z in self.order(NZ):
            self.sums[z] = run
            run = run + self.planes[z]
        waits = []
        for d in FAR_FIRST:
            z = lax.rem(me.z + d, NZ)
            waits.append(self.go(remote(
                self.sums.at[z], self.base.at[me.z], *self.sem(24 + d), me.at(z=z)
            )))
        self.base[me.z] = self.sums[me.z]
        for copy in waits:
            copy.wait_recv()

    def y_back(self):
        me = self.me
        base = self.base[...].reshape(HEAD, HEAD)
        waits = []
        for d in (2, 1, 3):
            y = lax.rem(me.y + d, NY)
            self.out[y] = self.ahead[y] + base
            waits.append((d, self.go(remote(
                self.out.at[y], self.mine.at[me.y], *self.sem(40 + d), me.at(y=y)
            ))))
        self.mine[me.y] = self.ahead[me.y] + base
        first = 1 if self.reverse else 0
        for d, copy in [(0, None)] + waits:
            s = lax.rem(me.y - d + NY, NY)
            if copy is not None:
                copy.wait_recv()
            head = HALF * me.core + s
            got = self.mine[s]
            leads = me.core == first
            self.fore[s] = got + jnp.where(leads, self.state[head], 0.0)
            self.result[head] = got + jnp.where(leads, 0.0, self.other[s])
            self.go(remote(
                self.fore.at[s], self.result.at[head], *self.sem(44 + d), me.at(core=1 - me.core)
            ))

    def result_slot(self, i):
        me = self.me
        d = (0, 2, 1, 3)[i % HALF]
        s = lax.rem(me.y - d + NY, NY)
        if i < HALF:
            return HALF * me.core + s
        head = HALF * (1 - me.core) + s
        remote(
            self.fore.at[s], self.result.at[head], *self.sem(44 + d), me.at(core=1 - me.core)
        ).wait_recv()
        return head

    def finish(self):
        for copy in self.sends:
            copy.wait_send()


def columns(head):
    if isinstance(head, int):
        return pl.ds(head * HEAD, HEAD)
    return pl.ds(pl.multiple_of(head * HEAD, HEAD), HEAD)


def kernel(
    q_hbm, k_hbm, v_hbm, gain_ref, g_hbm, dq_hbm, dk_hbm, dv_hbm,
    q_raw, k_raw, v_b, g_raw, q_b, k_b, q_inv, k_inv, att, wei, d_b, scores_b, dk_part, dv_part,
    prior_s, own_s, sums_s, dq_o, dk_o, dv_o, load_sems, store_sems, x_sems, *scan_bufs,
):
    me = Place()
    loads = [
        pltpu.make_async_copy(src, dst, load_sems.at[i])
        for i, (src, dst) in enumerate(((k_hbm, k_raw), (v_hbm, v_b), (q_hbm, q_raw), (g_hbm, g_raw)))
    ]
    for copy in loads:
        copy.start()
    barrier = pltpu.get_barrier_semaphore()
    peers = [me.at(core=1 - me.core)]
    peers += [me.at(z=lax.rem(me.z + d, NZ)) for d in FAR_FIRST]
    peers += [me.at(y=lax.rem(me.y + d, NY)) for d in (2, 1, 3)]
    peers += [me.at(x=lax.rem(me.x + d, NX)) for d in (2, 1, 3)]
    for peer in peers:
        pl.semaphore_signal(barrier, inc=1, device_id=peer, device_id_type=MESH)

    count = len(scan_bufs) // 2
    fore = Scan(me, own_s.at[0], scan_bufs[:count], False)
    back = Scan(me, own_s.at[1], scan_bufs[count:], True)

    def send_order(i):
        s = lax.rem(me.y + (1, 2, 3, 0)[i % HALF], NY)
        return s + HALF * ((1 - me.core) if i < HALF else me.core)

    loads[0].wait()
    loads[1].wait()
    for i in range(HEADS):
        head = send_order(i)
        cols = columns(head)
        wide = k_raw[:, cols].astype(F32)
        inv = lax.rsqrt(jnp.sum(wide * wide, -1, keepdims=True) + 1e-06)
        k_inv[head] = jnp.broadcast_to(inv, (BLOCK, HEAD))
        unit = (wide * inv).astype(BF16)
        k_b[:, cols] = unit
        own_s[0, head] = dot(unit, v_b[:, cols], TN)
    pl.semaphore_wait(barrier, len(peers))
    for d in (1, 2, 3, 0):
        fore.send_head(d)
    fore.y_phase()
    fore.z_send()

    loads[2].wait()
    loads[3].wait()
    lower = lax.broadcasted_iota(jnp.int32, (BLOCK, BLOCK), 0) >= lax.broadcasted_iota(jnp.int32, (BLOCK, BLOCK), 1)
    for head in range(HEADS):
        cols = columns(head)
        wide = q_raw[:, cols].astype(F32)
        inv = lax.rsqrt(jnp.sum(wide * wide, -1, keepdims=True) + 1e-06)
        q_inv[head] = jnp.broadcast_to(inv, (BLOCK, HEAD))
        unit = (wide * inv).astype(BF16)
        q_b[:, cols] = unit
        scores = jnp.where(lower, dot(unit, k_b[:, cols], NT), 0.0).astype(BF16)
        scores_b[head] = scores
        att[head] = dot(scores, v_b[:, cols], NN)
        wei[head] = g_raw[:, cols].astype(F32) * gain_ref[:, cols]
    fore.z_back()
    fore.y_back()

    square = jnp.zeros((BLOCK, HEAD), F32)
    cross = jnp.zeros((BLOCK, HEAD), F32)
    for i in range(HEADS):
        head = fore.result_slot(i)
        both = split(fore.result[head], 0)
        prior_s[head] = both
        out = att[head] + dot(twice(q_b[:, columns(head)]), both, NN)
        att[head] = out
        square = square + out * out
        cross = cross + wei[head] * out
    lane = lax.broadcasted_iota(jnp.int32, (BLOCK, HEAD), 1)
    pair = jnp.where(
        lane == 0, jnp.sum(square, -1, keepdims=True), jnp.sum(cross, -1, keepdims=True)
    )
    sums_s[0] = pair.T[:8]
    x_waits = []
    for d in (2, 1, 3):
        copy = remote(
            sums_s.at[0], sums_s.at[d], x_sems.at[0, d], x_sems.at[1, d], me.at(x=lax.rem(me.x + d, NX))
        )
        copy.start()
        x_waits.append(copy)
    for copy in x_waits:
        copy.wait_recv()
    total = (sums_s[0] + sums_s[1]) + (sums_s[2] + sums_s[3])
    full = NX * HEADS * HEAD
    scale = lax.rsqrt(total[0:1] / full + 1e-05)
    slope = total[1:2] * (scale * scale * scale) / full
    row = lax.broadcasted_iota(jnp.int32, (HEAD, BLOCK), 0)
    factors = jnp.where(row == 0, scale, slope).T
    scale, slope = factors[:, 0:1], factors[:, 1:2]

    for i in range(HEADS):
        head = send_order(i)
        cols = columns(head)
        grad = (wei[head] * scale - att[head] * slope).astype(BF16)
        d_b[:, cols] = grad
        own_s[1, head] = dot(q_b[:, cols], grad, TN)
        if i < HALF:
            back.send_head((1, 2, 3, 0)[i])
    back.y_phase()
    back.z_send()

    for head in range(HEADS):
        cols = columns(head)
        grad = d_b[:, cols]
        keys = k_b[:, cols]
        d_scores = jnp.where(lower, dot(grad, v_b[:, cols], NT), 0.0).astype(BF16)
        d_q = dot(d_scores, keys, NN)
        both = prior_s[head]
        d_q = d_q + dot(twice(grad), jnp.concatenate([both[:HEAD], both[HEAD:]], 1), NT)
        inv = q_inv[head]
        unit = q_raw[:, cols].astype(F32) * inv
        d_q = (d_q - unit * jnp.sum(unit * d_q, -1, keepdims=True)) * inv
        dq_o[:, cols] = d_q.astype(BF16)
        dk_part[head] = dot(d_scores, q_b[:, cols], TN)
        dv_part[head] = dot(scores_b[head], grad, TN)
    stores = [pltpu.make_async_copy(dq_o, dq_hbm, store_sems.at[0])]
    stores[0].start()
    back.z_back()
    back.y_back()

    for i in range(HEADS):
        head = back.result_slot(i)
        cols = columns(head)
        state = back.result[head]
        keys = k_b[:, cols]
        d_v = dv_part[head] + dot(twice(keys), split(state, 0), NN)
        dv_o[:, cols] = d_v.astype(BF16)
        d_k = dk_part[head] + dot(twice(v_b[:, cols]), split(state, 1), NT)
        inv = k_inv[head]
        unit = k_raw[:, cols].astype(F32) * inv
        d_k = (d_k - unit * jnp.sum(unit * d_k, -1, keepdims=True)) * inv
        dk_o[:, cols] = d_k.astype(BF16)
    stores.append(pltpu.make_async_copy(dk_o, dk_hbm, store_sems.at[1]))
    stores.append(pltpu.make_async_copy(dv_o, dv_hbm, store_sems.at[2]))
    for copy in stores[1:]:
        copy.start()
    fore.finish()
    back.finish()
    for copy in x_waits:
        copy.wait_send()
    for copy in stores:
        copy.wait()


def scan_scratch():
    square = pltpu.VMEM((HALF, HEAD, HEAD), F32)
    pieces = pltpu.VMEM((NZ, ROWS, HEAD), F32)
    return [
        square, square, square, square, pieces, pieces, pieces, pieces, square, square, square,
        pltpu.VMEM((HEADS, HEAD, HEAD), F32), pltpu.SemaphoreType.DMA((2, 48)),
    ]


def body(query, key, value, gain, grad_out):
    rows, width = query.shape
    flat = pltpu.VMEM((rows, width), BF16)
    wide = pltpu.VMEM((HEADS, rows, HEAD), F32)
    out = jax.ShapeDtypeStruct((rows, width), BF16)
    hbm = pl.BlockSpec(memory_space=pl.ANY)
    vmem = pl.BlockSpec(memory_space=pltpu.VMEM)
    return pl.pallas_call(
        kernel,
        out_shape=(out, out, out),
        in_specs=[hbm, hbm, hbm, vmem, hbm],
        out_specs=(hbm, hbm, hbm),
        scratch_shapes=[
            flat, flat, flat, flat, flat, flat, wide, wide, wide, wide, flat,
            pltpu.VMEM((HEADS, rows, rows), BF16), wide, wide,
            pltpu.VMEM((HEADS, 2 * HEAD, HEAD), BF16),
            pltpu.VMEM((2, HEADS, HEAD, HEAD), F32),
            pltpu.VMEM((NX, 8, rows), F32),
            flat, flat, flat,
            pltpu.SemaphoreType.DMA((4,)), pltpu.SemaphoreType.DMA((3,)), pltpu.SemaphoreType.DMA((2, NX)),
        ] + scan_scratch() + scan_scratch(),
        compiler_params=pltpu.CompilerParams(
            collective_id=0, has_side_effects=True, vmem_limit_bytes=40 << 20
        ),
        name="linear_attention_backward",
    )(query, key, value, gain.reshape(1, width), grad_out)


def solution(mesh):
    placed = (P("ctx", "tp"), P("ctx", "tp"), P("ctx", "tp"), P("tp"), P("ctx", "tp"))
    return jax.shard_map(
        body,
        mesh=mesh,
        in_specs=placed,
        out_specs=(P("ctx", "tp"), P("ctx", "tp"), P("ctx", "tp")),
        check_vma=False,
    )
```

time: 410 us -> 85.7 us (0.21)
  the two profiles are of different devices: /device:TPU:33 before, /device:TPU:1 now
where the time goes in v1:
time: 85.7 us; the launch traced here: 85.3 us
  Pallas kernels  77.5 us (90%)
  local copies, waits for them, and re-layouts  7.23 us (8%)
    pallas_call x1, Pallas kernels, body(): pl.pallas_call(kernel, out_shape=(out, out, out), in_specs=[hbm, hbm, hbm...  77.5 us
    unnamed x13, local copies, waits for them, and re-layouts  7.23 us

profile of v1, /device:TPU:1, one launch (start us, length us, event | category | flops | bytes accessed | tf_op | source)
XLA Modules:
  0.0 85.3 jit_solution(1020768464246416839)
XLA Ops:
  0.6 0.0 copy-start
  0.6 1.0 %copy-done = bf16[256,1024]{1,0:T(8,128)(2,1)S(1)} copy-done((bf16[256,1024]{1,0:T(8,128)(2,1)S(1)}, bf16[256,1024]{1,0:T(8,128)(2,1)}, u32[]{:S(2)}) %copy-start) | copy-done | bytes 524312
  1.7 0.0 copy-start.1
  1.7 1.0 %copy-done.1 = bf16[256,1024]{1,0:T(8,128)(2,1)S(1)} copy-done((bf16[256,1024]{1,0:T(8,128)(2,1)S(1)}, bf16[256,1024]{1,0:T(8,128)(2,1)}, u32[]{:S(2)}) %copy-start.1) | copy-done | bytes 524312
  2.7 0.0 copy-start.2
  2.7 1.0 %copy-done.2 = bf16[256,1024]{1,0:T(8,128)(2,1)S(1)} copy-done((bf16[256,1024]{1,0:T(8,128)(2,1)S(1)}, bf16[256,1024]{1,0:T(8,128)(2,1)}, u32[]{:S(2)}) %copy-start.2) | copy-done | bytes 524312
  3.8 0.0 copy-start.3
  3.8 1.0 %copy-done.3 = bf16[256,1024]{1,0:T(8,128)(2,1)S(1)} copy-done((bf16[256,1024]{1,0:T(8,128)(2,1)S(1)}, bf16[256,1024]{1,0:T(8,128)(2,1)}, u32[]{:S(2)}) %copy-start.3) | copy-done | bytes 524312
  4.8 0.0 copy-start.4
  4.8 0.7 copy-done.4
  5.5 77.5 %linear_attention_backward.1 = (bf16[256,1024]{1,0:T(8,128)(2,1)S(1)}, bf16[256,1024]{1,0:T(8,128)(2,1)S(1)}, bf16[256,1024]{1,0:T(8,128)(2,1)S(1)}) custom-call(bf16[256,1024]{1,0:T(8,128)(2,1)S(1)} %copy-done, bf16[256,1024]{1,0:T(8,128)(2,1)S(1)} %copy-done.1, bf16[256,1024]{1,0:T(8,128)(2,1)S(1)} %copy-done.2, f32[1,1024]{1,0:T(1,128)S(1)} %bitcast.1, ...), custom_call_target="tpu_custom_call" | custom-call | tf_op jit(solution)/shard_map/linear_attention_backward/pallas_call | solution.py:352
  83.0 0.8 copy.11
  83.7 0.8 copy.12
  84.5 0.8 copy.13
Async XLA Ops:
  0.6 1.0 %copy-start = (bf16[256,1024]{1,0:T(8,128)(2,1)S(1)}, bf16[256,1024]{1,0:T(8,128)(2,1)}, u32[]{:S(2)}) copy-start(bf16[256,1024]{1,0:T(8,128)(2,1)} %q_hbm.1) | copy-start | bytes 1572868
  1.7 1.0 %copy-start.1 = (bf16[256,1024]{1,0:T(8,128)(2,1)S(1)}, bf16[256,1024]{1,0:T(8,128)(2,1)}, u32[]{:S(2)}) copy-start(bf16[256,1024]{1,0:T(8,128)(2,1)} %k_hbm.1) | copy-start | bytes 1572868
  2.7 1.0 %copy-start.2 = (bf16[256,1024]{1,0:T(8,128)(2,1)S(1)}, bf16[256,1024]{1,0:T(8,128)(2,1)}, u32[]{:S(2)}) copy-start(bf16[256,1024]{1,0:T(8,128)(2,1)} %v_hbm.1) | copy-start | bytes 1572868
  3.8 1.0 %copy-start.3 = (bf16[256,1024]{1,0:T(8,128)(2,1)S(1)}, bf16[256,1024]{1,0:T(8,128)(2,1)}, u32[]{:S(2)}) copy-start(bf16[256,1024]{1,0:T(8,128)(2,1)} %g_hbm.1) | copy-start | bytes 1572868
  4.8 0.7 copy-start.4

commit v2 on v1

--- a/solution.py
+++ b/solution.py
@@ -12,11 +12,17 @@
 NY = 4
 NZ = 16
 NX = 4
-ROWS = HEAD // NZ
+SLICES = 8
+DEPTH = HEAD // SLICES
+CHUNKS = 2
+PART = SLICES // CHUNKS
 F32 = jnp.float32
 BF16 = jnp.bfloat16
 MESH = pl.DeviceIdType.MESH
 FAR_FIRST = sorted(range(1, NZ), key=lambda d: -min(d, NZ - d))
+BACK_SLOT = {e: (2 - e) % SLICES for e in range(-4, 4)}
+SHARE_ORDER = (0, 1, 3, 2)
+SEND_ORDER = (2, 1, 3, 0)
 
 NN = (((1,), (0,)), ((), ()))
 NT = (((1,), (1,)), ((), ()))
@@ -59,15 +65,21 @@
     )
 
 
+def hops(d):
+    return min(d % NZ, -d % NZ)
+
+
+def shift(slot):
+    return (slot + 6) % SLICES
+
+
 class Scan:
     def __init__(self, me, state, bufs, reverse):
         (self.other, self.chip, self.plane, self.ahead, self.total, self.planes, self.sums, self.base,
-         self.out, self.mine, self.fore, self.result, self.sems) = bufs
+         self.out, self.mine, self.fore, self.result, self.core_sems, self.y_sems, self.z_sems, self.zb_sems,
+         self.yb_sems, self.share_sems) = bufs
         self.me, self.state, self.reverse = me, state, reverse
         self.sends = []
-
-    def sem(self, slot):
-        return self.sems.at[0, slot], self.sems.at[1, slot]
 
     def order(self, count):
         return reversed(range(count)) if self.reverse else range(count)
@@ -77,102 +89,159 @@
         self.sends.append(copy)
         return copy
 
+    def slice_at(self, slot):
+        return lax.rem(self.me.z + shift(slot), SLICES)
+
+    def slot_of(self, j):
+        return lax.rem(2 * SLICES + j - 6 - lax.rem(self.me.z, SLICES), SLICES)
+
     def head_copy(self, d):
         me = self.me
         s = lax.rem(me.y + d, NY)
         return remote(
-            self.state.at[HALF * (1 - me.core) + s], self.other.at[s], *self.sem(d), me.at(core=1 - me.core)
+            self.state.at[HALF * (1 - me.core) + s], self.other.at[s], self.core_sems.at[0, d],
+            self.core_sems.at[1, d], me.at(core=1 - me.core)
         )
 
     def send_head(self, d):
         self.go(self.head_copy(d))
 
-    def y_phase(self):
-        me = self.me
-        waits = []
-        for d in (1, 2, 3, 0):
-            s = lax.rem(me.y + d, NY)
-            self.head_copy(d).wait_recv()
-            whole = self.state[HALF * me.core + s] + self.other[s]
-            if d:
-                self.chip[s] = whole
-                waits.append(self.go(remote(
-                    self.chip.at[s], self.plane.at[me.y], *self.sem(4 + d), me.at(y=s)
-                )))
-            else:
-                self.plane[s] = whole
-        for copy in waits:
-            copy.wait_recv()
-        run = jnp.zeros((HEAD, HEAD), F32)
-        for y in self.order(NY):
-            self.ahead[y] = run
-            run = run + self.plane[y]
-        self.total[...] = run.reshape(NZ, ROWS, HEAD)
+    def y_copy(self, chunk, d):
+        me = self.me
+        s = lax.rem(me.y + d, NY)
+        part = pl.ds(chunk * PART, PART)
+        return remote(
+            self.chip.at[s, part], self.plane.at[me.y, part], self.y_sems.at[0, chunk, d],
+            self.y_sems.at[1, chunk, d], me.at(y=s)
+        )
+
+    def y_send(self):
+        me = self.me
+        for chunk in range(CHUNKS):
+            for d in (2, 1, 3, 0):
+                s = lax.rem(me.y + d, NY)
+                if chunk == 0:
+                    self.head_copy(d).wait_recv()
+                for slot in range(chunk * PART, chunk * PART + PART):
+                    j = self.slice_at(slot)
+                    whole = self.state[HALF * me.core + s, j] + self.other[s, j]
+                    if d:
+                        self.chip[s, slot] = whole
+                    else:
+                        self.plane[me.y, slot] = whole
+                if d:
+                    self.go(self.y_copy(chunk, d))
+
+    def z_copy(self, slot, d):
+        me = self.me
+        d = d % NZ
+        z = lax.rem(me.z + d, NZ)
+        return remote(
+            self.total.at[slot], self.planes.at[me.z], self.z_sems.at[0, d], self.z_sems.at[1, d], me.at(z=z)
+        )
 
     def z_send(self):
         me = self.me
-        self.z_waits = []
-        for d in FAR_FIRST:
-            z = lax.rem(me.z + d, NZ)
-            self.z_waits.append(self.go(remote(
-                self.total.at[z], self.planes.at[me.z], *self.sem(8 + d), me.at(z=z)
-            )))
-        self.planes[me.z] = self.total[me.z]
+        for chunk in range(CHUNKS):
+            for d in (1, 3, 2):
+                self.y_copy(chunk, d).wait_recv()
+            slots = range(chunk * PART, chunk * PART + PART)
+            for slot in slots:
+                run = jnp.zeros((DEPTH, HEAD), F32)
+                for y in self.order(NY):
+                    self.ahead[y, slot] = run
+                    run = run + self.plane[y, slot]
+                self.total[slot] = run
+            targets = [(slot, shift(slot) + far) for slot in slots for far in (0, SLICES)]
+            for slot, d in sorted(targets, key=lambda t: -hops(t[1])):
+                if d:
+                    self.go(self.z_copy(slot, d))
+                else:
+                    self.planes[me.z] = self.total[slot]
+
+    def zb_copy(self, e):
+        me = self.me
+        z = lax.rem(me.z + e + NZ, NZ)
+        return remote(
+            self.sums.at[z], self.base.at[BACK_SLOT[e]], self.zb_sems.at[0, BACK_SLOT[e]],
+            self.zb_sems.at[1, BACK_SLOT[e]], me.at(z=z)
+        )
 
     def z_back(self):
         me = self.me
-        for copy in self.z_waits:
-            copy.wait_recv()
-        run = jnp.zeros((ROWS, HEAD), F32)
+        for d in sorted(range(1, NZ), key=hops):
+            self.z_copy(0, d).wait_recv()
+        run = jnp.zeros((DEPTH, HEAD), F32)
         for z in self.order(NZ):
             self.sums[z] = run
             run = run + self.planes[z]
-        waits = []
-        for d in FAR_FIRST:
-            z = lax.rem(me.z + d, NZ)
-            waits.append(self.go(remote(
-                self.sums.at[z], self.base.at[me.z], *self.sem(24 + d), me.at(z=z)
-            )))
-        self.base[me.z] = self.sums[me.z]
-        for copy in waits:
-            copy.wait_recv()
+        for e in sorted(BACK_SLOT, key=lambda e: -abs(e)):
+            if e:
+                self.go(self.zb_copy(e))
+        self.base[BACK_SLOT[0]] = self.sums[me.z]
+
+    def yb_copy(self, chunk, d):
+        me = self.me
+        y = lax.rem(me.y + d, NY)
+        part = pl.ds(chunk * PART, PART)
+        return remote(
+            self.out.at[y, part], self.mine.at[me.y, part], self.yb_sems.at[0, chunk, d],
+            self.yb_sems.at[1, chunk, d], me.at(y=y)
+        )
+
+    def share_copy(self, chunk, d):
+        me = self.me
+        s = lax.rem(me.y - d + NY, NY)
+        part = pl.ds(chunk * PART, PART)
+        return remote(
+            self.fore.at[s, part], self.result.at[HALF * me.core + s, part], self.share_sems.at[0, chunk, d],
+            self.share_sems.at[1, chunk, d], me.at(core=1 - me.core)
+        )
 
     def y_back(self):
         me = self.me
-        base = self.base[...].reshape(HEAD, HEAD)
-        waits = []
-        for d in (2, 1, 3):
-            y = lax.rem(me.y + d, NY)
-            self.out[y] = self.ahead[y] + base
-            waits.append((d, self.go(remote(
-                self.out.at[y], self.mine.at[me.y], *self.sem(40 + d), me.at(y=y)
-            ))))
-        self.mine[me.y] = self.ahead[me.y] + base
-        first = 1 if self.reverse else 0
-        for d, copy in [(0, None)] + waits:
-            s = lax.rem(me.y - d + NY, NY)
-            if copy is not None:
-                copy.wait_recv()
-            head = HALF * me.core + s
-            got = self.mine[s]
-            leads = me.core == first
-            self.fore[s] = got + jnp.where(leads, self.state[head], 0.0)
-            self.result[head] = got + jnp.where(leads, 0.0, self.other[s])
-            self.go(remote(
-                self.fore.at[s], self.result.at[head], *self.sem(44 + d), me.at(core=1 - me.core)
-            ))
-
-    def result_slot(self, i):
-        me = self.me
-        d = (0, 2, 1, 3)[i % HALF]
+        leads = me.core == (1 if self.reverse else 0)
+        for chunk in range(CHUNKS):
+            slots = range(chunk * PART, chunk * PART + PART)
+            for e, slot in sorted(BACK_SLOT.items(), key=lambda t: abs(t[0])):
+                if e and slot in slots:
+                    self.zb_copy(e).wait_recv()
+            for d in (2, 1, 3, 0):
+                y = lax.rem(me.y + d, NY)
+                for slot in slots:
+                    value = self.ahead[y, slot] + self.base[slot]
+                    if d:
+                        self.out[y, slot] = value
+                    else:
+                        self.mine[y, slot] = value
+                if d:
+                    self.go(self.yb_copy(chunk, d))
+        for chunk in range(CHUNKS):
+            slots = range(chunk * PART, chunk * PART + PART)
+            for d in SHARE_ORDER:
+                if d:
+                    self.yb_copy(chunk, d).wait_recv()
+                s = lax.rem(me.y - d + NY, NY)
+                head = HALF * me.core + s
+                for slot in slots:
+                    j = self.slice_at(slot)
+                    got = self.mine[s, slot]
+                    self.fore[s, slot] = got + jnp.where(leads, self.state[head, j], 0.0)
+                    self.result[head, slot] = got + jnp.where(leads, 0.0, self.other[s, j])
+                self.go(self.share_copy(chunk, d))
+
+    def result_head(self, i):
+        me = self.me
+        d = SHARE_ORDER[i % HALF]
         s = lax.rem(me.y - d + NY, NY)
         if i < HALF:
             return HALF * me.core + s
-        head = HALF * (1 - me.core) + s
-        remote(
-            self.fore.at[s], self.result.at[head], *self.sem(44 + d), me.at(core=1 - me.core)
-        ).wait_recv()
-        return head
+        for chunk in range(CHUNKS):
+            self.share_copy(chunk, d).wait_recv()
+        return HALF * (1 - me.core) + s
+
+    def result_state(self, head):
+        return jnp.concatenate([self.result[head, self.slot_of(j)] for j in range(SLICES)], 0)
 
     def finish(self):
         for copy in self.sends:
@@ -186,14 +255,14 @@
 
 
 def kernel(
-    q_hbm, k_hbm, v_hbm, gain_ref, g_hbm, dq_hbm, dk_hbm, dv_hbm,
-    q_raw, k_raw, v_b, g_raw, q_b, k_b, q_inv, k_inv, att, wei, d_b, scores_b, dk_part, dv_part,
+    q_hbm, k_hbm, v_hbm, gain_hbm, g_hbm, dq_hbm, dk_hbm, dv_hbm,
+    q_raw, k_raw, v_b, g_raw, gain_ref, q_b, k_b, q_inv, k_inv, att, wei, d_b, scores_b, dk_part, dv_part,
     prior_s, own_s, sums_s, dq_o, dk_o, dv_o, load_sems, store_sems, x_sems, *scan_bufs,
 ):
     me = Place()
     loads = [
         pltpu.make_async_copy(src, dst, load_sems.at[i])
-        for i, (src, dst) in enumerate(((k_hbm, k_raw), (v_hbm, v_b), (q_hbm, q_raw), (g_hbm, g_raw)))
+        for i, (src, dst) in enumerate(((k_hbm, k_raw), (v_hbm, v_b), (q_hbm, q_raw), (g_hbm, g_raw), (gain_hbm, gain_ref)))
     ]
     for copy in loads:
         copy.start()
@@ -210,7 +279,7 @@
     back = Scan(me, own_s.at[1], scan_bufs[count:], True)
 
     def send_order(i):
-        s = lax.rem(me.y + (1, 2, 3, 0)[i % HALF], NY)
+        s = lax.rem(me.y + SEND_ORDER[i % HALF], NY)
         return s + HALF * ((1 - me.core) if i < HALF else me.core)
 
     loads[0].wait()
@@ -223,15 +292,16 @@
         k_inv[head] = jnp.broadcast_to(inv, (BLOCK, HEAD))
         unit = (wide * inv).astype(BF16)
         k_b[:, cols] = unit
-        own_s[0, head] = dot(unit, v_b[:, cols], TN)
+        own_s[0, head] = dot(unit, v_b[:, cols], TN).reshape(SLICES, DEPTH, HEAD)
     pl.semaphore_wait(barrier, len(peers))
-    for d in (1, 2, 3, 0):
+    for d in SEND_ORDER:
         fore.send_head(d)
-    fore.y_phase()
+    fore.y_send()
     fore.z_send()
 
     loads[2].wait()
     loads[3].wait()
+    loads[4].wait()
     lower = lax.broadcasted_iota(jnp.int32, (BLOCK, BLOCK), 0) >= lax.broadcasted_iota(jnp.int32, (BLOCK, BLOCK), 1)
     for head in range(HEADS):
         cols = columns(head)
@@ -250,8 +320,8 @@
     square = jnp.zeros((BLOCK, HEAD), F32)
     cross = jnp.zeros((BLOCK, HEAD), F32)
     for i in range(HEADS):
-        head = fore.result_slot(i)
-        both = split(fore.result[head], 0)
+        head = fore.result_head(i)
+        both = split(fore.result_state(head), 0)
         prior_s[head] = both
         out = att[head] + dot(twice(q_b[:, columns(head)]), both, NN)
         att[head] = out
@@ -284,10 +354,10 @@
         cols = columns(head)
         grad = (wei[head] * scale - att[head] * slope).astype(BF16)
         d_b[:, cols] = grad
-        own_s[1, head] = dot(q_b[:, cols], grad, TN)
+        own_s[1, head] = dot(q_b[:, cols], grad, TN).reshape(SLICES, DEPTH, HEAD)
         if i < HALF:
-            back.send_head((1, 2, 3, 0)[i])
-    back.y_phase()
+            back.send_head(SEND_ORDER[i])
+    back.y_send()
     back.z_send()
 
     for head in range(HEADS):
@@ -310,9 +380,9 @@
     back.y_back()
 
     for i in range(HEADS):
-        head = back.result_slot(i)
+        head = back.result_head(i)
         cols = columns(head)
-        state = back.result[head]
+        state = back.result_state(head)
         keys = k_b[:, cols]
         d_v = dv_part[head] + dot(twice(keys), split(state, 0), NN)
         dv_o[:, cols] = d_v.astype(BF16)
@@ -334,11 +404,15 @@
 
 
 def scan_scratch():
-    square = pltpu.VMEM((HALF, HEAD, HEAD), F32)
-    pieces = pltpu.VMEM((NZ, ROWS, HEAD), F32)
+    heads = pltpu.VMEM((HALF, SLICES, DEPTH, HEAD), F32)
+    slices = pltpu.VMEM((SLICES, DEPTH, HEAD), F32)
+    along_z = pltpu.VMEM((NZ, DEPTH, HEAD), F32)
+    sems = pltpu.SemaphoreType.DMA
     return [
-        square, square, square, square, pieces, pieces, pieces, pieces, square, square, square,
-        pltpu.VMEM((HEADS, HEAD, HEAD), F32), pltpu.SemaphoreType.DMA((2, 48)),
+        heads, heads, heads, heads, slices, along_z, along_z, slices, heads, heads, heads,
+        pltpu.VMEM((HEADS, SLICES, DEPTH, HEAD), F32),
+        sems((2, NY)), sems((2, CHUNKS, NY)), sems((2, NZ)), sems((2, SLICES)), sems((2, CHUNKS, NY)),
+        sems((2, CHUNKS, NY)),
     ]
 
 
@@ -348,26 +422,26 @@
     wide = pltpu.VMEM((HEADS, rows, HEAD), F32)
     out = jax.ShapeDtypeStruct((rows, width), BF16)
     hbm = pl.BlockSpec(memory_space=pl.ANY)
-    vmem = pl.BlockSpec(memory_space=pltpu.VMEM)
-    return pl.pallas_call(
+    grads = pl.pallas_call(
         kernel,
         out_shape=(out, out, out),
-        in_specs=[hbm, hbm, hbm, vmem, hbm],
+        in_specs=[hbm] * 5,
         out_specs=(hbm, hbm, hbm),
         scratch_shapes=[
-            flat, flat, flat, flat, flat, flat, wide, wide, wide, wide, flat,
+            flat, flat, flat, flat, pltpu.VMEM((1, width), F32), flat, flat, wide, wide, wide, wide, flat,
             pltpu.VMEM((HEADS, rows, rows), BF16), wide, wide,
             pltpu.VMEM((HEADS, 2 * HEAD, HEAD), BF16),
-            pltpu.VMEM((2, HEADS, HEAD, HEAD), F32),
+            pltpu.VMEM((2, HEADS, SLICES, DEPTH, HEAD), F32),
             pltpu.VMEM((NX, 8, rows), F32),
             flat, flat, flat,
-            pltpu.SemaphoreType.DMA((4,)), pltpu.SemaphoreType.DMA((3,)), pltpu.SemaphoreType.DMA((2, NX)),
+            pltpu.SemaphoreType.DMA((5,)), pltpu.SemaphoreType.DMA((3,)), pltpu.SemaphoreType.DMA((2, NX)),
         ] + scan_scratch() + scan_scratch(),
         compiler_params=pltpu.CompilerParams(
-            collective_id=0, has_side_effects=True, vmem_limit_bytes=40 << 20
+            collective_id=0, has_side_effects=True, vmem_limit_bytes=52 << 20
         ),
         name="linear_attention_backward",
     )(query, key, value, gain.reshape(1, width), grad_out)
+    return grads
 
 
 def solution(mesh):

time: 85.7 us -> 77.2 us (0.901)
  local copies, waits for them, and re-layouts: 7.23 us -> 3.06 us
  Pallas kernels: 77.5 us -> 73.4 us
    unnamed x13 -> x5, local copies, waits for them, and re-layouts: 7.23 us -> 3.06 us
    pallas_call x1, Pallas kernels: 77.5 us -> 73.4 us  [body(): pl.pallas_call(kernel, out_shape=(out, out, out), in_specs=[hbm] * 5, out...]
where the time goes in v2:
time: 77.2 us; the launch traced here: 77.1 us
  Pallas kernels  73.4 us (95%)
  local copies, waits for them, and re-layouts  3.06 us (4%)
    pallas_call x1, Pallas kernels, body(): pl.pallas_call(kernel, out_shape=(out, out, out), in_specs=[hbm] * 5, out...  73.4 us
    unnamed x5, local copies, waits for them, and re-layouts  3.06 us

profile of v2, /device:TPU:1, one launch (start us, length us, event | category | flops | bytes accessed | tf_op | source)
XLA Modules:
  0.0 77.1 jit_solution(6840720518104814593)
XLA Ops:
  0.6 0.0 copy-start
  0.6 0.7 copy-done
  1.3 73.4 %linear_attention_backward.1 = (bf16[256,1024]{1,0:T(8,128)(2,1)S(1)}, bf16[256,1024]{1,0:T(8,128)(2,1)S(1)}, bf16[256,1024]{1,0:T(8,128)(2,1)S(1)}) custom-call(bf16[256,1024]{1,0:T(8,128)(2,1)} %q_hbm.1, bf16[256,1024]{1,0:T(8,128)(2,1)} %k_hbm.1, bf16[256,1024]{1,0:T(8,128)(2,1)} %v_hbm.1, f32[1,1024]{1,0:T(1,128)S(1)} %bitcast.1, bf16[256,1024]{1,0:T(8,128)(2,1)} %g_hbm.1), custom_call_target="tpu_custom_call" | custom-call | tf_op jit(solution)/shard_map/linear_attention_backward/pallas_call | solution.py:425
  74.7 0.8 %copy.11 = bf16[256,1024]{1,0:T(8,128)(2,1)} copy(bf16[256,1024]{1,0:T(8,128)(2,1)S(1)} %get-tuple-element.6) | data formatting | bytes 1048576
  75.5 0.8 %copy.12 = bf16[256,1024]{1,0:T(8,128)(2,1)} copy(bf16[256,1024]{1,0:T(8,128)(2,1)S(1)} %get-tuple-element.7) | data formatting | bytes 1048576
  76.3 0.8 %copy.13 = bf16[256,1024]{1,0:T(8,128)(2,1)} copy(bf16[256,1024]{1,0:T(8,128)(2,1)S(1)} %get-tuple-element.8) | data formatting | bytes 1048576
Async XLA Ops:
  0.6 0.7 copy-start

commit v3 on v2

--- a/solution.py
+++ b/solution.py
@@ -13,6 +13,7 @@
 NZ = 16
 NX = 4
 SLICES = 8
+REACH = 4
 DEPTH = HEAD // SLICES
 CHUNKS = 2
 PART = SLICES // CHUNKS
@@ -256,19 +257,21 @@
 
 def kernel(
     q_hbm, k_hbm, v_hbm, gain_hbm, g_hbm, dq_hbm, dk_hbm, dv_hbm,
-    q_raw, k_raw, v_b, g_raw, gain_ref, q_b, k_b, q_inv, k_inv, att, wei, d_b, scores_b, dk_part, dv_part,
-    prior_s, own_s, sums_s, dq_o, dk_o, dv_o, load_sems, store_sems, x_sems, *scan_bufs,
+    q_raw, k_raw, v_b, g_raw, gain_ref, q_t, q_b, k_b, q_inv, k_inv, att, wei, d_b, scores_b, dk_part, dv_part,
+    prior_s, own_s, sums_s, dq_o, dk_o, dv_o, load_sems, store_sems, x_sems, relay, *scan_bufs,
 ):
     me = Place()
-    loads = [
-        pltpu.make_async_copy(src, dst, load_sems.at[i])
-        for i, (src, dst) in enumerate(((k_hbm, k_raw), (v_hbm, v_b), (q_hbm, q_raw), (g_hbm, g_raw), (gain_hbm, gain_ref)))
-    ]
+    pairs = []
+    for core in (1 - me.core, me.core):
+        cols = pl.ds(pl.multiple_of(core * HALF * HEAD, HEAD), HALF * HEAD)
+        pairs += [(k_hbm.at[:, cols], k_raw.at[:, cols]), (v_hbm.at[:, cols], v_b.at[:, cols])]
+    pairs += [(q_hbm, q_raw), (g_hbm, g_raw), (gain_hbm, gain_ref)]
+    loads = [pltpu.make_async_copy(src, dst, load_sems.at[i]) for i, (src, dst) in enumerate(pairs)]
     for copy in loads:
         copy.start()
     barrier = pltpu.get_barrier_semaphore()
     peers = [me.at(core=1 - me.core)]
-    peers += [me.at(z=lax.rem(me.z + d, NZ)) for d in FAR_FIRST]
+    peers += [me.at(z=lax.rem(me.z + d, NZ)) for d in FAR_FIRST if hops(d) <= REACH]
     peers += [me.at(y=lax.rem(me.y + d, NY)) for d in (2, 1, 3)]
     peers += [me.at(x=lax.rem(me.x + d, NX)) for d in (2, 1, 3)]
     for peer in peers:
@@ -282,9 +285,10 @@
         s = lax.rem(me.y + SEND_ORDER[i % HALF], NY)
         return s + HALF * ((1 - me.core) if i < HALF else me.core)
 
-    loads[0].wait()
-    loads[1].wait()
     for i in range(HEADS):
+        if i % HALF == 0:
+            loads[i // HALF * 2].wait()
+            loads[i // HALF * 2 + 1].wait()
         head = send_order(i)
         cols = columns(head)
         wide = k_raw[:, cols].astype(F32)
@@ -293,15 +297,21 @@
         unit = (wide * inv).astype(BF16)
         k_b[:, cols] = unit
         own_s[0, head] = dot(unit, v_b[:, cols], TN).reshape(SLICES, DEPTH, HEAD)
-    pl.semaphore_wait(barrier, len(peers))
-    for d in SEND_ORDER:
-        fore.send_head(d)
+        if i == HALF - 1:
+            pl.semaphore_wait(barrier, len(peers))
+            for side, d in enumerate((REACH, NZ - REACH)):
+                pl.semaphore_signal(
+                    relay.at[side], inc=1, device_id=me.at(z=lax.rem(me.z + d, NZ)), device_id_type=MESH
+                )
+            for d in SEND_ORDER:
+                fore.send_head(d)
     fore.y_send()
+    for side in range(2):
+        pl.semaphore_wait(relay.at[side], 1)
     fore.z_send()
 
-    loads[2].wait()
-    loads[3].wait()
-    loads[4].wait()
+    for copy in loads[4:]:
+        copy.wait()
     lower = lax.broadcasted_iota(jnp.int32, (BLOCK, BLOCK), 0) >= lax.broadcasted_iota(jnp.int32, (BLOCK, BLOCK), 1)
     for head in range(HEADS):
         cols = columns(head)
@@ -310,6 +320,7 @@
         q_inv[head] = jnp.broadcast_to(inv, (BLOCK, HEAD))
         unit = (wide * inv).astype(BF16)
         q_b[:, cols] = unit
+        q_t[head] = unit.T
         scores = jnp.where(lower, dot(unit, k_b[:, cols], NT), 0.0).astype(BF16)
         scores_b[head] = scores
         att[head] = dot(scores, v_b[:, cols], NN)
@@ -354,7 +365,7 @@
         cols = columns(head)
         grad = (wei[head] * scale - att[head] * slope).astype(BF16)
         d_b[:, cols] = grad
-        own_s[1, head] = dot(q_b[:, cols], grad, TN).reshape(SLICES, DEPTH, HEAD)
+        own_s[1, head] = dot(q_t[head], grad, NN).reshape(SLICES, DEPTH, HEAD)
         if i < HALF:
             back.send_head(SEND_ORDER[i])
     back.y_send()
@@ -428,13 +439,14 @@
         in_specs=[hbm] * 5,
         out_specs=(hbm, hbm, hbm),
         scratch_shapes=[
-            flat, flat, flat, flat, pltpu.VMEM((1, width), F32), flat, flat, wide, wide, wide, wide, flat,
+            flat, flat, flat, flat, pltpu.VMEM((1, width), F32), pltpu.VMEM((HEADS, HEAD, rows), BF16), flat, flat, wide, wide, wide, wide, flat,
             pltpu.VMEM((HEADS, rows, rows), BF16), wide, wide,
             pltpu.VMEM((HEADS, 2 * HEAD, HEAD), BF16),
             pltpu.VMEM((2, HEADS, SLICES, DEPTH, HEAD), F32),
             pltpu.VMEM((NX, 8, rows), F32),
             flat, flat, flat,
-            pltpu.SemaphoreType.DMA((5,)), pltpu.SemaphoreType.DMA((3,)), pltpu.SemaphoreType.DMA((2, NX)),
+            pltpu.SemaphoreType.DMA((7,)), pltpu.SemaphoreType.DMA((3,)), pltpu.SemaphoreType.DMA((2, NX)),
+            pltpu.SemaphoreType.REGULAR((2,)),
         ] + scan_scratch() + scan_scratch(),
         compiler_params=pltpu.CompilerParams(
             collective_id=0, has_side_effects=True, vmem_limit_bytes=52 << 20

time: 77.2 us -> 75.2 us (0.974)
  Pallas kernels: 73.4 us -> 71.4 us
    pallas_call x1, Pallas kernels: 73.4 us -> 71.4 us  [body(): pl.pallas_call(kernel, out_shape=(out, out, out), in_specs=[hbm] * 5, out...]
where the time goes in v3:
time: 75.2 us; the launch traced here: 75.1 us
  Pallas kernels  71.4 us (95%)
  local copies, waits for them, and re-layouts  3.06 us (4%)
    pallas_call x1, Pallas kernels, body(): pl.pallas_call(kernel, out_shape=(out, out, out), in_specs=[hbm] * 5, out...  71.4 us
    unnamed x5, local copies, waits for them, and re-layouts  3.06 us

profile of v3, /device:TPU:1, one launch (start us, length us, event | category | flops | bytes accessed | tf_op | source)
XLA Modules:
  0.0 75.1 jit_solution(12093756976993454946)
XLA Ops:
  0.6 0.0 copy-start
  0.6 0.7 copy-done
  1.3 71.4 %linear_attention_backward.1 = (bf16[256,1024]{1,0:T(8,128)(2,1)S(1)}, bf16[256,1024]{1,0:T(8,128)(2,1)S(1)}, bf16[256,1024]{1,0:T(8,128)(2,1)S(1)}) custom-call(bf16[256,1024]{1,0:T(8,128)(2,1)} %q_hbm.1, bf16[256,1024]{1,0:T(8,128)(2,1)} %k_hbm.1, bf16[256,1024]{1,0:T(8,128)(2,1)} %v_hbm.1, f32[1,1024]{1,0:T(1,128)S(1)} %bitcast.1, bf16[256,1024]{1,0:T(8,128)(2,1)} %g_hbm.1), custom_call_target="tpu_custom_call" | custom-call | tf_op jit(solution)/shard_map/linear_attention_backward/pallas_call | solution.py:436
  72.7 0.8 %copy.11 = bf16[256,1024]{1,0:T(8,128)(2,1)} copy(bf16[256,1024]{1,0:T(8,128)(2,1)S(1)} %get-tuple-element.6) | data formatting | bytes 1048576
  73.5 0.8 %copy.12 = bf16[256,1024]{1,0:T(8,128)(2,1)} copy(bf16[256,1024]{1,0:T(8,128)(2,1)S(1)} %get-tuple-element.7) | data formatting | bytes 1048576
  74.3 0.8 %copy.13 = bf16[256,1024]{1,0:T(8,128)(2,1)} copy(bf16[256,1024]{1,0:T(8,128)(2,1)S(1)} %get-tuple-element.8) | data formatting | bytes 1048576
Async XLA Ops:
  0.6 0.7 copy-start

commit v4 on v3

--- a/solution.py
+++ b/solution.py
@@ -13,7 +13,7 @@
 NZ = 16
 NX = 4
 SLICES = 8
-REACH = 4
+REACH = (2, 4)
 DEPTH = HEAD // SLICES
 CHUNKS = 2
 PART = SLICES // CHUNKS
@@ -217,6 +217,7 @@
                         self.mine[y, slot] = value
                 if d:
                     self.go(self.yb_copy(chunk, d))
+        self.drain()
         for chunk in range(CHUNKS):
             slots = range(chunk * PART, chunk * PART + PART)
             for d in SHARE_ORDER:
@@ -244,9 +245,22 @@
     def result_state(self, head):
         return jnp.concatenate([self.result[head, self.slot_of(j)] for j in range(SLICES)], 0)
 
-    def finish(self):
+    def drain(self):
         for copy in self.sends:
             copy.wait_send()
+        self.sends = []
+
+
+def vouch(me, relay, step):
+    for side, d in enumerate((REACH[step], NZ - REACH[step])):
+        pl.semaphore_signal(
+            relay.at[step, side], inc=1, device_id=me.at(z=lax.rem(me.z + d, NZ)), device_id_type=MESH
+        )
+
+
+def heard(relay, step):
+    for side in range(2):
+        pl.semaphore_wait(relay.at[step, side], 1)
 
 
 def columns(head):
@@ -256,9 +270,9 @@
 
 
 def kernel(
-    q_hbm, k_hbm, v_hbm, gain_hbm, g_hbm, dq_hbm, dk_hbm, dv_hbm,
+    q_hbm, k_hbm, v_hbm, gain_hbm, g_hbm, dq_o, dk_o, dv_o,
     q_raw, k_raw, v_b, g_raw, gain_ref, q_t, q_b, k_b, q_inv, k_inv, att, wei, d_b, scores_b, dk_part, dv_part,
-    prior_s, own_s, sums_s, dq_o, dk_o, dv_o, load_sems, store_sems, x_sems, relay, *scan_bufs,
+    prior_s, own_s, sums_s, load_sems, x_sems, relay, *scan_bufs,
 ):
     me = Place()
     pairs = []
@@ -271,7 +285,7 @@
         copy.start()
     barrier = pltpu.get_barrier_semaphore()
     peers = [me.at(core=1 - me.core)]
-    peers += [me.at(z=lax.rem(me.z + d, NZ)) for d in FAR_FIRST if hops(d) <= REACH]
+    peers += [me.at(z=lax.rem(me.z + d, NZ)) for d in FAR_FIRST if hops(d) <= REACH[0]]
     peers += [me.at(y=lax.rem(me.y + d, NY)) for d in (2, 1, 3)]
     peers += [me.at(x=lax.rem(me.x + d, NX)) for d in (2, 1, 3)]
     for peer in peers:
@@ -299,15 +313,13 @@
         own_s[0, head] = dot(unit, v_b[:, cols], TN).reshape(SLICES, DEPTH, HEAD)
         if i == HALF - 1:
             pl.semaphore_wait(barrier, len(peers))
-            for side, d in enumerate((REACH, NZ - REACH)):
-                pl.semaphore_signal(
-                    relay.at[side], inc=1, device_id=me.at(z=lax.rem(me.z + d, NZ)), device_id_type=MESH
-                )
+            vouch(me, relay, 0)
             for d in SEND_ORDER:
                 fore.send_head(d)
+    heard(relay, 0)
+    vouch(me, relay, 1)
     fore.y_send()
-    for side in range(2):
-        pl.semaphore_wait(relay.at[side], 1)
+    heard(relay, 1)
     fore.z_send()
 
     for copy in loads[4:]:
@@ -385,8 +397,10 @@
         dq_o[:, cols] = d_q.astype(BF16)
         dk_part[head] = dot(d_scores, q_b[:, cols], TN)
         dv_part[head] = dot(scores_b[head], grad, TN)
-    stores = [pltpu.make_async_copy(dq_o, dq_hbm, store_sems.at[0])]
-    stores[0].start()
+    fore.drain()
+    for copy in x_waits:
+        copy.wait_send()
+    back.drain()
     back.z_back()
     back.y_back()
 
@@ -402,16 +416,7 @@
         unit = k_raw[:, cols].astype(F32) * inv
         d_k = (d_k - unit * jnp.sum(unit * d_k, -1, keepdims=True)) * inv
         dk_o[:, cols] = d_k.astype(BF16)
-    stores.append(pltpu.make_async_copy(dk_o, dk_hbm, store_sems.at[1]))
-    stores.append(pltpu.make_async_copy(dv_o, dv_hbm, store_sems.at[2]))
-    for copy in stores[1:]:
-        copy.start()
-    fore.finish()
-    back.finish()
-    for copy in x_waits:
-        copy.wait_send()
-    for copy in stores:
-        copy.wait()
+    back.drain()
 
 
 def scan_scratch():
@@ -437,16 +442,15 @@
         kernel,
         out_shape=(out, out, out),
         in_specs=[hbm] * 5,
-        out_specs=(hbm, hbm, hbm),
+        out_specs=(pl.BlockSpec(memory_space=pltpu.VMEM),) * 3,
         scratch_shapes=[
             flat, flat, flat, flat, pltpu.VMEM((1, width), F32), pltpu.VMEM((HEADS, HEAD, rows), BF16), flat, flat, wide, wide, wide, wide, flat,
             pltpu.VMEM((HEADS, rows, rows), BF16), wide, wide,
             pltpu.VMEM((HEADS, 2 * HEAD, HEAD), BF16),
             pltpu.VMEM((2, HEADS, SLICES, DEPTH, HEAD), F32),
             pltpu.VMEM((NX, 8, rows), F32),
-            flat, flat, flat,
-            pltpu.SemaphoreType.DMA((7,)), pltpu.SemaphoreType.DMA((3,)), pltpu.SemaphoreType.DMA((2, NX)),
-            pltpu.SemaphoreType.REGULAR((2,)),
+            pltpu.SemaphoreType.DMA((7,)), pltpu.SemaphoreType.DMA((2, NX)),
+            pltpu.SemaphoreType.REGULAR((2, 2)),
         ] + scan_scratch() + scan_scratch(),
         compiler_params=pltpu.CompilerParams(
             collective_id=0, has_side_effects=True, vmem_limit_bytes=52 << 20

time: 75.2 us -> 74 us (0.984)
  Pallas kernels: 71.4 us -> 70.1 us
    pallas_call x1, Pallas kernels: 71.4 us -> 70.1 us  [body(): pl.pallas_call(kernel, out_shape=(out, out, out), in_specs=[hbm] * 5, out...]
where the time goes in v4:
time: 74 us; the launch traced here: 73.9 us
  Pallas kernels  70.1 us (95%)
  local copies, waits for them, and re-layouts  3.06 us (4%)
    pallas_call x1, Pallas kernels, body(): pl.pallas_call(kernel, out_shape=(out, out, out), in_specs=[hbm] * 5, out...  70.1 us
    unnamed x5, local copies, waits for them, and re-layouts  3.06 us

profile of v4, /device:TPU:1, one launch (start us, length us, event | category | flops | bytes accessed | tf_op | source)
XLA Modules:
  0.0 73.9 jit_solution(7802480922768820420)
XLA Ops:
  0.6 0.0 copy-start
  0.6 0.7 copy-done
  1.3 70.1 %linear_attention_backward.1 = (bf16[256,1024]{1,0:T(8,128)(2,1)S(1)}, bf16[256,1024]{1,0:T(8,128)(2,1)S(1)}, bf16[256,1024]{1,0:T(8,128)(2,1)S(1)}) custom-call(bf16[256,1024]{1,0:T(8,128)(2,1)} %q_hbm.1, bf16[256,1024]{1,0:T(8,128)(2,1)} %k_hbm.1, bf16[256,1024]{1,0:T(8,128)(2,1)} %v_hbm.1, f32[1,1024]{1,0:T(1,128)S(1)} %bitcast.1, bf16[256,1024]{1,0:T(8,128)(2,1)} %g_hbm.1), custom_call_target="tpu_custom_call" | custom-call | tf_op jit(solution)/shard_map/linear_attention_backward/pallas_call | solution.py:441
  71.5 0.8 %copy.11 = bf16[256,1024]{1,0:T(8,128)(2,1)} copy(bf16[256,1024]{1,0:T(8,128)(2,1)S(1)} %get-tuple-element.6) | data formatting | bytes 1048576
  72.3 0.8 %copy.12 = bf16[256,1024]{1,0:T(8,128)(2,1)} copy(bf16[256,1024]{1,0:T(8,128)(2,1)S(1)} %get-tuple-element.7) | data formatting | bytes 1048576
  73.1 0.8 %copy.13 = bf16[256,1024]{1,0:T(8,128)(2,1)} copy(bf16[256,1024]{1,0:T(8,128)(2,1)S(1)} %get-tuple-element.8) | data formatting | bytes 1048576
Async XLA Ops:
  0.6 0.7 copy-start

commit v5 on v4

--- a/solution.py
+++ b/solution.py
@@ -14,6 +14,7 @@
 NX = 4
 SLICES = 8
 REACH = (2, 4)
+LEAST = 4
 DEPTH = HEAD // SLICES
 CHUNKS = 2
 PART = SLICES // CHUNKS
@@ -143,6 +144,7 @@
 
     def z_send(self):
         me = self.me
+        targets = []
         for chunk in range(CHUNKS):
             for d in (1, 3, 2):
                 self.y_copy(chunk, d).wait_recv()
@@ -153,8 +155,10 @@
                     self.ahead[y, slot] = run
                     run = run + self.plane[y, slot]
                 self.total[slot] = run
-            targets = [(slot, shift(slot) + far) for slot in slots for far in (0, SLICES)]
-            for slot, d in sorted(targets, key=lambda t: -hops(t[1])):
+            targets += [(slot, shift(slot) + far) for slot in slots for far in (0, SLICES)]
+            ready = [t for t in targets if hops(t[1]) >= LEAST or chunk == CHUNKS - 1]
+            targets = [t for t in targets if t not in ready]
+            for slot, d in sorted(ready, key=lambda t: -hops(t[1])):
                 if d:
                     self.go(self.z_copy(slot, d))
                 else:

time: 74 us -> 73.6 us (level)
  no operation moved by 1% of the time
where the time goes in v5:
time: 73.6 us; the launch traced here: 73.4 us
  Pallas kernels  69.7 us (95%)
  local copies, waits for them, and re-layouts  3.06 us (4%)
    pallas_call x1, Pallas kernels, body(): pl.pallas_call(kernel, out_shape=(out, out, out), in_specs=[hbm] * 5, out...  69.7 us
    unnamed x5, local copies, waits for them, and re-layouts  3.06 us

profile of v5, /device:TPU:1, one launch (start us, length us, event | category | flops | bytes accessed | tf_op | source)
XLA Modules:
  0.0 73.4 jit_solution(15305447163591702696)
XLA Ops:
  0.6 0.0 copy-start
  0.6 0.7 copy-done
  1.3 69.7 %linear_attention_backward.1 = (bf16[256,1024]{1,0:T(8,128)(2,1)S(1)}, bf16[256,1024]{1,0:T(8,128)(2,1)S(1)}, bf16[256,1024]{1,0:T(8,128)(2,1)S(1)}) custom-call(bf16[256,1024]{1,0:T(8,128)(2,1)} %q_hbm.1, bf16[256,1024]{1,0:T(8,128)(2,1)} %k_hbm.1, bf16[256,1024]{1,0:T(8,128)(2,1)} %v_hbm.1, f32[1,1024]{1,0:T(1,128)S(1)} %bitcast.1, bf16[256,1024]{1,0:T(8,128)(2,1)} %g_hbm.1), custom_call_target="tpu_custom_call" | custom-call | tf_op jit(solution)/shard_map/linear_attention_backward/pallas_call | solution.py:445
  71.0 0.8 %copy.11 = bf16[256,1024]{1,0:T(8,128)(2,1)} copy(bf16[256,1024]{1,0:T(8,128)(2,1)S(1)} %get-tuple-element.6) | data formatting | bytes 1048576
  71.8 0.8 %copy.12 = bf16[256,1024]{1,0:T(8,128)(2,1)} copy(bf16[256,1024]{1,0:T(8,128)(2,1)S(1)} %get-tuple-element.7) | data formatting | bytes 1048576
  72.6 0.8 %copy.13 = bf16[256,1024]{1,0:T(8,128)(2,1)} copy(bf16[256,1024]{1,0:T(8,128)(2,1)S(1)} %get-tuple-element.8) | data formatting | bytes 1048576
Async XLA Ops:
  0.6 0.7 copy-start
